TPU v7x, 256 devices: a whole 4x4x8 slice. The times are simulated.
256 devices in a mesh: seq: 32 (over z, x_hi, core), head: 8 (over x_lo, y).
Axes of the slice: x: 4 (x_hi: 2, x_lo: 2; x = x_hi * 2 + x_lo), y: 4, z: 8, core: 2. Of those that a mesh axis runs over, the one named last changes fastest.
Arguments:
- queries: bfloat16 [4, 65536, 1024], P(None, 'seq', 'head'), may hold values from -6 to 6
- keys_values: bfloat16 [4, 65536, 2, 1024], P(None, 'seq', None, 'head'), may hold values from -720 to 720
- norm_gain: float32 [1024], P('head'), may hold values from 0.1 to 1.9
Outputs:
- normalized: bfloat16 [4, 65536, 1024], P(None, 'seq', 'head')
All inputs are finite; a program needn't handle non-finite values.
Results may differ from a plain program's by a relative error of at most 0.005.
Values may be sent and summed in bfloat16 or wider, within the bound.
A program may use at most 64 MiB of HBM per device.

v0:
```python
from functools import reduce
import math

import jax
import jax.numpy as jnp
from jax import lax
from jax.sharding import PartitionSpec as P

HD = 128
P_SIZE = 16


def with_halo(block, sides, width):
    for axis, dim in sides:
        count = lax.axis_size(axis)
        forward = [(i, i + 1) for i in range(count - 1)]
        backward = [(target, source) for source, target in forward]
        low = lax.ppermute(
            lax.slice_in_dim(block, block.shape[dim] - width, None, axis=dim), axis, forward
        )
        high = lax.ppermute(lax.slice_in_dim(block, 0, width, axis=dim), axis, backward)
        block = jnp.concatenate([low, block, high], axis=dim)
    return block


def pool(source):
    batch_size, cells = (source.shape[0], source.shape[1])
    grouped = source.reshape(
        batch_size, cells // P_SIZE, P_SIZE, source.shape[2], source.shape[3]
    ).astype(jnp.float32)
    return (jnp.sum(grouped, axis=2) / P_SIZE).astype(jnp.bfloat16)


def attend(query_block, key_groups, query_pos, group_pos, seq_length):
    block_len = P_SIZE * P_SIZE
    margin_len = block_len // 2
    cube_len = P_SIZE**3
    block_start = query_pos // block_len * block_len
    near_lo = block_start - margin_len
    near_hi = block_start + block_len + margin_len
    first_lo = block_start - 2 * block_len
    first_hi = block_start + 3 * block_len
    second_lo = first_lo // cube_len * cube_len - cube_len
    second_hi = -(-first_hi // cube_len) * cube_len + cube_len

    def inside(positions, lower, upper):
        return (positions[None, :] >= lower[:, None]) & (positions[None, :] < upper[:, None])

    def present(positions):
        return ((positions >= 0) & (positions < seq_length))[None, :]

    key_masks = [
        inside(group_pos[0], near_lo, near_hi) & present(group_pos[0]),
        inside(group_pos[1], first_lo, first_hi)
        & ~inside(group_pos[1], near_lo, near_hi)
        & present(group_pos[1]),
        inside(group_pos[2], second_lo, second_hi)
        & ~inside(group_pos[2], first_lo, first_hi)
        & present(group_pos[2]),
        ~inside(group_pos[3], second_lo, second_hi) & present(group_pos[3]),
    ]
    head_dim = query_block.shape[-1]
    scores = []
    for level_num in range(4):
        raw_score = jnp.einsum(
            "sqhe,skhe->shqk",
            query_block,
            key_groups[level_num][:, :, 0],
            preferred_element_type=jnp.float32,
        )
        shifted = raw_score / math.sqrt(head_dim) + level_num * math.log(P_SIZE) / 2
        scores.append(jnp.where(key_masks[level_num][None, None], shifted, -jnp.inf))
    row_max = reduce(jnp.maximum, [jnp.max(score, axis=-1) for score in scores])
    totals = []
    products = []
    for level_num in range(4):
        weight = jnp.exp(scores[level_num] - row_max[..., None])
        totals.append(jnp.sum(weight, axis=-1))
        products.append(
            jnp.einsum(
                "shqk,skhe->sqhe",
                weight.astype(jnp.bfloat16),
                key_groups[level_num][:, :, 1],
                preferred_element_type=jnp.float32,
            )
        )
    row_total = totals[0] + totals[1] + totals[2] + totals[3]
    weighted = products[0] + products[1] + products[2] + products[3]
    return (weighted / jnp.transpose(row_total, (0, 2, 1))[..., None]).astype(jnp.bfloat16)


def on_device(queries, keys_values, norm_gain):
    batch_size, tok_rows, local_width = queries.shape
    head_count = local_width // HD
    devices_seq = lax.axis_size("seq")
    seq_index = lax.axis_index("seq")
    seq_length = tok_rows * devices_seq
    dev_start = seq_index * tok_rows
    block_len = P_SIZE * P_SIZE
    margin_len = block_len // 2
    cube_len = P_SIZE**3
    level_one = pool(keys_values)
    level_two = pool(level_one)
    near_pad = with_halo(keys_values, (("seq", 1),), margin_len)
    one_pad = with_halo(level_one, (("seq", 1),), 2 * P_SIZE)
    second_level = lax.all_gather(level_two, "seq", axis=1, tiled=True)
    second_pos = jnp.arange(second_level.shape[1], dtype=jnp.int32) * block_len
    level_three = pool(second_level)
    three_pos = jnp.arange(seq_length // cube_len, dtype=jnp.int32) * cube_len

    def split_heads(source):
        return source.reshape(batch_size, source.shape[1], 2, head_count, HD)

    second_heads = split_heads(second_level)
    three_heads = split_heads(level_three)
    query_heads = queries.reshape(batch_size, tok_rows, head_count, HD)
    query_rows = min(512, tok_rows)
    block_count = tok_rows // query_rows

    def do_block(block_num, output_buf):
        query_off = block_num * query_rows
        query_block = lax.dynamic_slice_in_dim(query_heads, query_off, query_rows, 1)
        near_keys = split_heads(
            lax.dynamic_slice_in_dim(near_pad, query_off, query_rows + 2 * margin_len, 1)
        )
        near_pos = (
            dev_start
            + query_off
            - margin_len
            + jnp.arange(query_rows + 2 * margin_len, dtype=jnp.int32)
        )
        first_keys = split_heads(
            lax.dynamic_slice_in_dim(
                one_pad, query_off // P_SIZE, query_rows // P_SIZE + 4 * P_SIZE, 1
            )
        )
        first_pos = (
            dev_start
            + query_off
            - 2 * block_len
            + jnp.arange(query_rows // P_SIZE + 4 * P_SIZE, dtype=jnp.int32) * P_SIZE
        )
        query_pos = dev_start + query_off + jnp.arange(query_rows, dtype=jnp.int32)
        result = attend(
            query_block,
            [near_keys, first_keys, second_heads, three_heads],
            query_pos,
            [near_pos, first_pos, second_pos, three_pos],
            seq_length,
        )
        return lax.dynamic_update_slice_in_dim(
            output_buf, result.reshape(batch_size, query_rows, local_width), query_off, 1
        )

    attention = lax.fori_loop(
        0, block_count, do_block, jnp.zeros((batch_size, tok_rows, local_width), jnp.bfloat16)
    )
    attention_wide = attention.astype(jnp.float32)
    square = jnp.sum(attention_wide * attention_wide, axis=-1)
    square_sum = lax.psum(square, "head")
    full_width = local_width * lax.axis_size("head")
    scale_row = 1.0 / jnp.sqrt(square_sum / full_width + 1e-06)
    return (attention_wide * scale_row[..., None] * norm_gain).astype(jnp.bfloat16)


def solution(mesh):
    in_specs = (P(None, "seq", "head"), P(None, "seq", None, "head"), P("head"))
    out_specs = P(None, "seq", "head")
    return jax.shard_map(
        on_device, mesh=mesh, in_specs=in_specs, out_specs=out_specs, check_vma=False
    )
```

profile of v0, /device:TPU:100, one launch (start us, length us, event | category | flops | bytes accessed | tf_op | source)
XLA Modules:
  0.0 180.8 jit_solution(5390324567490346371)
XLA Ops:
  0.0 8.8 %convert_reduce_fusion = f32[4,128,2,128]{3,2,1,0:T(2,128)S(1)} fusion(bf16[4,128,16,2,128]{4,3,2,1,0:T(2,128)(2,1)} %bitcast.124), kind=kLoop, calls=%fused_computation.116 | loop fusion | flops 4063232 | bytes 4718592 | tf_op jit(solution)/shard_map/reduce_sum | solution.py:31
  9.1 1.9 %collective-permute-start.2 = (bf16[4,32,2,128]{3,2,1,0:T(2,128)(2,1)S(1)}, bf16[4,32,2,128]{3,2,1,0:T(2,128)(2,1)S(1)}, u32[]{:S(2)}, u32[]{:S(2)}) collective-permute-start(bf16[4,32,2,128]{3,2,1,0:T(2,128)(2,1)S(1)} %get-tuple-element.425), channel_id=1, source_target_pairs={{0,8},{8,16},{16,24},{24,32},{32,40},{40,48},{48,56},{56,64},{64,7... | collective-permute-start | bytes 196616 | tf_op jit(solution)/shard_map/ppermute | solution.py:18
  11.1 5.1 %collective-permute-start.3 = (bf16[4,32,2,128]{3,2,1,0:T(2,128)(2,1)S(1)}, bf16[4,32,2,128]{3,2,1,0:T(2,128)(2,1)S(1)}, u32[]{:S(2)}, u32[]{:S(2)}) collective-permute-start(bf16[4,32,2,128]{3,2,1,0:T(2,128)(2,1)S(1)} %get-tuple-element.426), channel_id=1, source_target_pairs={{8,0},{16,8},{24,16},{32,24},{40,32},{48,40},{56,48},{64,56},{72,6... | collective-permute-start | bytes 196616 | tf_op jit(solution)/shard_map/ppermute | solution.py:21
  16.2 0.5 copy.35
  16.8 2.0 %copy-done = bf16[4,2048,2,128]{3,1,0,2:T(8,128)(2,1)} copy-done((bf16[4,2048,2,128]{3,1,0,2:T(8,128)(2,1)}, bf16[4,2048,2,128]{3,1,0,2:T(8,128)(2,1)S(1)}, u32[]{:S(2)}) %copy-start) | copy-done | bytes 4194328
  18.8 1.9 %collective-permute-start = (bf16[4,128,2,128]{3,1,0,2:T(8,128)(2,1)S(1)}, bf16[4,128,2,128]{3,1,0,2:T(8,128)(2,1)S(1)}, u32[]{:S(2)}, u32[]{:S(2)}) collective-permute-start(bf16[4,128,2,128]{3,1,0,2:T(8,128)(2,1)S(1)} %get-tuple-element.423), channel_id=1, source_target_pairs={{0,8},{8,16},{16,24},{24,32},{32,40},{40,48},{48,56},{56,64},{64,7... | collective-permute-start | bytes 786440 | tf_op jit(solution)/shard_map/ppermute | solution.py:18
  20.8 5.1 %collective-permute-start.1 = (bf16[4,128,2,128]{3,1,0,2:T(8,128)(2,1)S(1)}, bf16[4,128,2,128]{3,1,0,2:T(8,128)(2,1)S(1)}, u32[]{:S(2)}, u32[]{:S(2)}) collective-permute-start(bf16[4,128,2,128]{3,1,0,2:T(8,128)(2,1)S(1)} %get-tuple-element.424), channel_id=1, source_target_pairs={{8,0},{16,8},{24,16},{32,24},{40,32},{48,40},{56,48},{64,56},{72,6... | collective-permute-start | bytes 786440 | tf_op jit(solution)/shard_map/ppermute | solution.py:21
  26.2 43.2 %all_gather.3 = bf16[4,256,2,128]{3,2,1,0:T(2,128)(2,1)S(1)} all-gather(bf16[4,8,2,128]{3,2,1,0:T(2,128)(2,1)S(1)} %multiply_convert_fusion.2), channel_id=1, replica_groups=mesh['seq'=32,'head'=8] {'seq'}, dimensions={1}, use_global_device_ids=true | all-gather | bytes 540672 | tf_op jit(solution)/shard_map/all_gather | solution.py:106
  69.4 0.4 convert_reduce_fusion.1
  69.8 0.6 copy.40
  70.4 0.9 copy.39
  71.3 0.6 pad_maximum_fusion.1
  71.9 3.9 %pad_maximum_fusion = bf16[4,2304,2,128]{3,1,0,2:T(8,128)(2,1)} fusion(bf16[4,128,2,128]{3,1,0,2:T(8,128)(2,1)S(1)} %collective-permute-done.1, bf16[4,2048,2,128]{3,1,0,2:T(8,128)(2,1)} %copy-done, bf16[4,128,2,128]{3,1,0,2:T(8,128)(2,1)S(1)} %collective-permute-done), kind=kLoop, calls=%fused_computation.119 | loop fusion | flops 14155776 | bytes 9437184 | tf_op jit(solution)/shard_map/concatenate | solution.py:22
  76.1 65.9 %while.18 = (s32[]{:T(128)}, bf16[4,2048,128]{2,1,0:T(8,128)(2,1)S(1)}, bf16[4,2304,2,128]{3,1,0,2:T(8,128)(2,1)}, s32[]{:T(128)}, bf16[4,2048,1,128]{3,1,0,2:T(...) while((s32[]{:T(128)}, ...), condition=%wide.region_12.13_spmd.clone.clone, body=%wide.region_3.12_spmd.clone.clone.sunk | while | flops 1219108608 | bytes 55795316 | solution.py:155
  76.8 1.5 fusion.102
  78.5 0.4 and_and_fusion.6
  78.9 1.4 fusion.104
  80.3 1.5 dynamic-slice_bitcast_fusion.2
  81.9 1.5 fusion.103
  83.4 1.4 fusion.100
  84.9 2.2 %fusion.105 = f32[4,128,512]{2,1,0:T(8,128)S(1)} fusion(f32[4,512,768]{2,1,0:T(8,128)S(1)} %get-tuple-element.492, f32[4,512]{1,0:T(4,128)S(1)} %maximum_maximum_fusion.2, pred[512,768]{1,0:T(8,128)(4,1)S(1)} %and_and_fusion.6, bf16[4,768,2,1,128]{4,1,0,3,2:T(8,128)(2,1)S(1)} %dynamic-slice_bitcast_fusion.2), kind=kOutput, calls=%fused_computation.7.clone.1 | convolution fusion | flops 408944640 | bytes 8527872 | tf_op jit(solution)/shard_map/while/body/eval_jaxpr/shqk,skhe->sqhe/dot_general | solution.py:80
  87.1 1.8 fusion.109
  88.8 0.4 convolution_add_fusion.2
  89.3 1.4 fusion.106
  90.8 0.3 fusion.108
  91.1 1.1 fusion.111
  93.3 1.5 fusion.102
  95.0 0.4 and_and_fusion.6
  95.4 1.4 fusion.104
  96.8 1.5 dynamic-slice_bitcast_fusion.2
  98.4 1.5 fusion.103
  99.9 1.4 fusion.100
  101.3 2.2 %fusion.105 = f32[4,128,512]{2,1,0:T(8,128)S(1)} fusion(f32[4,512,768]{2,1,0:T(8,128)S(1)} %get-tuple-element.492, f32[4,512]{1,0:T(4,128)S(1)} %maximum_maximum_fusion.2, pred[512,768]{1,0:T(8,128)(4,1)S(1)} %and_and_fusion.6, bf16[4,768,2,1,128]{4,1,0,3,2:T(8,128)(2,1)S(1)} %dynamic-slice_bitcast_fusion.2), kind=kOutput, calls=%fused_computation.7.clone.1 | convolution fusion | flops 408944640 | bytes 8527872 | tf_op jit(solution)/shard_map/while/body/eval_jaxpr/shqk,skhe->sqhe/dot_general | solution.py:80
  103.6 1.8 fusion.109
  105.3 0.4 convolution_add_fusion.2
  105.8 1.4 fusion.106
  107.2 0.3 fusion.108
  107.6 1.1 fusion.111
  109.8 1.5 fusion.102
  111.5 0.4 and_and_fusion.6
  111.9 1.4 fusion.104
  113.3 1.5 dynamic-slice_bitcast_fusion.2
  114.8 1.5 fusion.103
  116.4 1.4 fusion.100
  117.8 2.2 %fusion.105 = f32[4,128,512]{2,1,0:T(8,128)S(1)} fusion(f32[4,512,768]{2,1,0:T(8,128)S(1)} %get-tuple-element.492, f32[4,512]{1,0:T(4,128)S(1)} %maximum_maximum_fusion.2, pred[512,768]{1,0:T(8,128)(4,1)S(1)} %and_and_fusion.6, bf16[4,768,2,1,128]{4,1,0,3,2:T(8,128)(2,1)S(1)} %dynamic-slice_bitcast_fusion.2), kind=kOutput, calls=%fused_computation.7.clone.1 | convolution fusion | flops 408944640 | bytes 8527872 | tf_op jit(solution)/shard_map/while/body/eval_jaxpr/shqk,skhe->sqhe/dot_general | solution.py:80
  120.0 1.8 fusion.109
  121.8 0.4 convolution_add_fusion.2
  122.3 1.4 fusion.106
  123.7 0.3 fusion.108
  124.1 1.1 fusion.111
  126.3 1.5 fusion.102
  127.9 0.4 and_and_fusion.6
  128.4 1.4 fusion.104
  129.8 1.5 dynamic-slice_bitcast_fusion.2
  131.3 1.5 fusion.103
  132.9 1.4 fusion.100
  134.3 2.2 %fusion.105 = f32[4,128,512]{2,1,0:T(8,128)S(1)} fusion(f32[4,512,768]{2,1,0:T(8,128)S(1)} %get-tuple-element.492, f32[4,512]{1,0:T(4,128)S(1)} %maximum_maximum_fusion.2, pred[512,768]{1,0:T(8,128)(4,1)S(1)} %and_and_fusion.6, bf16[4,768,2,1,128]{4,1,0,3,2:T(8,128)(2,1)S(1)} %dynamic-slice_bitcast_fusion.2), kind=kOutput, calls=%fused_computation.7.clone.1 | convolution fusion | flops 408944640 | bytes 8527872 | tf_op jit(solution)/shard_map/while/body/eval_jaxpr/shqk,skhe->sqhe/dot_general | solution.py:80
  136.5 1.8 fusion.109
  138.3 0.4 convolution_add_fusion.2
  138.8 1.4 fusion.106
  140.6 1.1 fusion.111
  142.0 1.2 fusion.67
  143.2 35.0 %psum.7 = f32[4,2048]{1,0:T(4,128)S(1)} all-reduce(f32[4,2048]{1,0:T(4,128)S(1)} %fusion.67), channel_id=1, replica_groups=mesh['seq'=32,'head'=8] {'head'}, use_global_device_ids=true, to_apply=%region_14.15 | all-reduce | flops 8192 | bytes 65536 | tf_op jit(solution)/shard_map/psum | solution.py:160
  178.2 2.6 %fusion.69 = bf16[4,2048,128]{2,1,0:T(8,128)(2,1)} fusion(bf16[4,2048,128]{2,1,0:T(8,128)(2,1)S(1)} %get-tuple-element.318, f32[128]{0:T(128)S(1)} %copy-done.3, f32[4,2048]{1,0:T(4,128)S(1)} %add_rsqrt_fusion), kind=kLoop, calls=%fused_computation.122 | loop fusion | flops 4194304 | bytes 4227584 | tf_op jit(solution)/shard_map/convert_element_type | solution.py:163
  (114 shorter events, 6.7 us)
Async XLA Ops:
  0.0 16.2 %copy-start.1 = (bf16[4,2048,2,128]{3,2,1,0:T(2,128)(2,1)S(1)}, bf16[4,2048,2,128]{3,2,1,0:T(2,128)(2,1)}, u32[]{:S(2)}) copy-start(bf16[4,2048,2,128]{3,2,1,0:T(2,128)(2,1)} %param.6) | copy-start | bytes 12582916
  9.1 62.2 %collective-permute-start.2 = (bf16[4,32,2,128]{3,2,1,0:T(2,128)(2,1)S(1)}, bf16[4,32,2,128]{3,2,1,0:T(2,128)(2,1)S(1)}, u32[]{:S(2)}, u32[]{:S(2)}) collective-permute-start(bf16[4,32,2,128]{3,2,1,0:T(2,128)(2,1)S(1)} %get-tuple-element.425), channel_id=1, source_target_pairs={{0,8},{8,16},{16,24},{24,32},{32,40},{40,48},{48,56},{56,64},{64,7... | collective-permute-start | bytes 196616 | tf_op jit(solution)/shard_map/ppermute | solution.py:18
  11.1 60.3 %collective-permute-start.3 = (bf16[4,32,2,128]{3,2,1,0:T(2,128)(2,1)S(1)}, bf16[4,32,2,128]{3,2,1,0:T(2,128)(2,1)S(1)}, u32[]{:S(2)}, u32[]{:S(2)}) collective-permute-start(bf16[4,32,2,128]{3,2,1,0:T(2,128)(2,1)S(1)} %get-tuple-element.426), channel_id=1, source_target_pairs={{8,0},{16,8},{24,16},{32,24},{40,32},{48,40},{56,48},{64,56},{72,6... | collective-permute-start | bytes 196616 | tf_op jit(solution)/shard_map/ppermute | solution.py:21
  16.8 2.0 %copy-start = (bf16[4,2048,2,128]{3,1,0,2:T(8,128)(2,1)}, bf16[4,2048,2,128]{3,1,0,2:T(8,128)(2,1)S(1)}, u32[]{:S(2)}) copy-start(bf16[4,2048,2,128]{3,1,0,2:T(8,128)(2,1)S(1)} %copy.35) | copy-start | bytes 12582916
  18.8 53.0 %collective-permute-start = (bf16[4,128,2,128]{3,1,0,2:T(8,128)(2,1)S(1)}, bf16[4,128,2,128]{3,1,0,2:T(8,128)(2,1)S(1)}, u32[]{:S(2)}, u32[]{:S(2)}) collective-permute-start(bf16[4,128,2,128]{3,1,0,2:T(8,128)(2,1)S(1)} %get-tuple-element.423), channel_id=1, source_target_pairs={{0,8},{8,16},{16,24},{24,32},{32,40},{40,48},{48,56},{56,64},{64,7... | collective-permute-start | bytes 786440 | tf_op jit(solution)/shard_map/ppermute | solution.py:18
  20.8 51.1 %collective-permute-start.1 = (bf16[4,128,2,128]{3,1,0,2:T(8,128)(2,1)S(1)}, bf16[4,128,2,128]{3,1,0,2:T(8,128)(2,1)S(1)}, u32[]{:S(2)}, u32[]{:S(2)}) collective-permute-start(bf16[4,128,2,128]{3,1,0,2:T(8,128)(2,1)S(1)} %get-tuple-element.424), channel_id=1, source_target_pairs={{8,0},{16,8},{24,16},{32,24},{40,32},{48,40},{56,48},{64,56},{72,6... | collective-permute-start | bytes 786440 | tf_op jit(solution)/shard_map/ppermute | solution.py:21
  76.1 102.2 %copy-start.3 = (f32[128]{0:T(128)S(1)}, f32[128]{0:T(128)}, u32[]{:S(2)}) copy-start(f32[128]{0:T(128)} %param.7) | copy-start | bytes 1540
  76.8 5.0 %copy-start.2 = (bf16[4,2048,1,128]{3,1,0,2:T(8,128)(2,1)S(1)}, bf16[4,2048,1,128]{3,1,0,2:T(8,128)(2,1)}, u32[]{:S(2)}) copy-start(bf16[4,2048,1,128]{3,1,0,2:T(8,128)(2,1)} %get-tuple-element.546) | copy-start | bytes 6291460 | tf_op jit(solution)/shard_map/while
  93.3 5.0 %copy-start.2 = (bf16[4,2048,1,128]{3,1,0,2:T(8,128)(2,1)S(1)}, bf16[4,2048,1,128]{3,1,0,2:T(8,128)(2,1)}, u32[]{:S(2)}) copy-start(bf16[4,2048,1,128]{3,1,0,2:T(8,128)(2,1)} %get-tuple-element.546) | copy-start | bytes 6291460 | tf_op jit(solution)/shard_map/while
  109.8 5.0 %copy-start.2 = (bf16[4,2048,1,128]{3,1,0,2:T(8,128)(2,1)S(1)}, bf16[4,2048,1,128]{3,1,0,2:T(8,128)(2,1)}, u32[]{:S(2)}) copy-start(bf16[4,2048,1,128]{3,1,0,2:T(8,128)(2,1)} %get-tuple-element.546) | copy-start | bytes 6291460 | tf_op jit(solution)/shard_map/while
  126.3 5.0 %copy-start.2 = (bf16[4,2048,1,128]{3,1,0,2:T(8,128)(2,1)S(1)}, bf16[4,2048,1,128]{3,1,0,2:T(8,128)(2,1)}, u32[]{:S(2)}) copy-start(bf16[4,2048,1,128]{3,1,0,2:T(8,128)(2,1)} %get-tuple-element.546) | copy-start | bytes 6291460 | tf_op jit(solution)/shard_map/while
where the time goes:
time: 183 us; the launch traced here: 181 us
  blocking collectives  78.2 us (43%)
  matrix products  43.5 us (24%)
  other arithmetic  31.2 us (17%)
  starting transfers between devices  14.1 us (8%)
  local copies, waits for them, and re-layouts  12.6 us (7%)
    all_gather x1, blocking collectives, on_device(): second_level = lax.all_gather(level_two, 'seq', axis=1, tiled=True)  43.2 us
    psum x1, blocking collectives, on_device(): square_sum = lax.psum(square, 'head')  35 us
    dot_general x16, matrix products, attend(): jnp.einsum('sqhe,skhe->shqk', query_block, key_groups[level_num][:, :, 0]...  23.3 us
    dot_general x16, matrix products, attend(): jnp.einsum('shqk,skhe->sqhe', weight.astype(jnp.bfloat16), key_groups[lev...  20.2 us
    ppermute x2, starting transfers between devices, with_halo(): lax.ppermute(lax.slice_in_dim(block, 0, width, axis=dim), axis, backward)  10.3 us
    reduce_sum x3, other arithmetic, pool(): return (jnp.sum(grouped, axis=2) / P_SIZE).astype(jnp.bfloat16)  9.42 us
    reduce_sum x16, other arithmetic, attend(): totals.append(jnp.sum(weight, axis=-1))  8.93 us
    reshape x4, local copies, waits for them, and re-layouts, split_heads(): return source.reshape(batch_size, source.shape[1], 2, head_count, HD)  6.11 us
  transfers between devices with their start and end apart: 4, of which 0 were waited for; matrix products, arithmetic and copies ran while one was open for 2% of the time, Pallas kernels for 0%

commit v1 on v0

v1 whole, which is shorter than its diff:
```python
import functools
import math

import jax
import jax.numpy as jnp
from jax import lax
from jax.experimental import pallas as pl
from jax.experimental.pallas import tpu as pltpu
from jax.sharding import PartitionSpec as P

HD = 128
CELL = 16
BLK = 256
CUBE = 4096
MARGIN = 128
NEAR = 512
LOW = 24
EXTRA = 128
ROWS = 272
NEG = -1e30
EXP_SCALE = math.log2(math.e) / math.sqrt(HD)
LEVEL_STEP = 2.0 / EXP_SCALE
MESH = pl.DeviceIdType.MESH
F32 = jnp.float32
BF16 = jnp.bfloat16


def dot_nt(a, b):
    return lax.dot_general(a, b, (((1,), (1,)), ((), ())), preferred_element_type=F32)


def dot_nn(a, b):
    return lax.dot_general(a, b, (((1,), (0,)), ((), ())), preferred_element_type=F32)


def iota(shape, dim):
    return lax.broadcasted_iota(jnp.int32, shape, dim)


def split_matrix():
    row = iota((ROWS, BLK), 0)
    col = iota((ROWS, BLK), 1)
    keys = (row < MARGIN) & (col == 2 * row)
    values = (row >= MARGIN) & (row < BLK) & (col == 2 * (row - MARGIN) + 1)
    cell = row - BLK
    pooled = (row >= BLK) & (col // (2 * CELL) == cell % 8) & (col % 2 == cell // 8)
    return jnp.where(
        keys | values, 1.0, jnp.where(pooled, 1.0 / CELL, 0.0)
    ).astype(BF16)


def fmm_kernel(
    n_seq,
    n_head,
    q_hbm,
    kv_hbm,
    att_hbm,
    total_hbm,
    raw,
    q_buf,
    k_buf,
    v_buf,
    k1,
    v1,
    k23,
    v23,
    tok_recv,
    cells_send,
    cells_recv,
    pair,
    cube_recv,
    third_send,
    third,
    att,
    own_sum,
    sums,
    total,
    splitter,
    q_sem,
    kv_sem,
    out_sem,
    tok_ssem,
    tok_rsem,
    cells_ssem,
    cells_rsem,
    pair_ssem,
    pair_rsem,
    cube_ssem,
    cube_rsem,
    third_ssem,
    third_rsem,
    sum_ssem,
    sum_rsem,
):
    seqs, toks, _ = q_hbm.shape
    blocks = toks // BLK
    cells = toks // CELL
    cubes = n_seq // 2
    seq_len = n_seq * toks
    me = lax.axis_index("seq")
    head = lax.axis_index("head")
    core = me % 2
    chip = me // 2
    dev_start = me * toks
    has_low = me > 0
    has_high = me < n_seq - 1

    for s in range(seqs):
        pltpu.make_async_copy(kv_hbm.at[s], raw.at[s], kv_sem.at[s]).start()
    for s in range(seqs):
        pltpu.make_async_copy(q_hbm.at[s], q_buf.at[s], q_sem.at[s]).start()

    barrier = pltpu.get_barrier_semaphore()

    def greet(seq_id, head_id):
        pl.semaphore_signal(
            barrier, inc=1, device_id=(seq_id, head_id), device_id_type=MESH
        )

    greet(me + 1 - 2 * core, head)
    for k in range(1, cubes):
        greet((chip + k) % cubes * 2 + core, head)
    for k in range(1, n_head):
        greet(me, (head + k) % n_head)
    outer = me - 1 + 2 * core
    outer_there = (outer >= 0) & (outer < n_seq)

    @pl.when(outer_there)
    def _():
        greet(outer, head)

    splitter[...] = split_matrix()
    v_buf[:, :, HD:] = jnp.ones((seqs, toks + BLK, HD), BF16)
    spare = 16 - (cubes - 1)
    third[(cubes - 1) * 8 :, :] = jnp.zeros((spare * 8, HD), F32)
    k23[...] = jnp.zeros_like(k23)
    v23[...] = jnp.zeros_like(v23)

    @pl.when(jnp.logical_not(has_low))
    def _():
        k_buf[:, :MARGIN, :] = jnp.zeros((seqs, MARGIN, HD), BF16)
        v_buf[:, :MARGIN, :HD] = jnp.zeros((seqs, MARGIN, HD), BF16)
        k1[:, :32, :] = jnp.zeros((seqs, 32, HD), F32)
        v1[:, :32, :] = jnp.zeros((seqs, 32, HD), F32)

    @pl.when(jnp.logical_not(has_high))
    def _():
        k_buf[:, MARGIN + toks :, :] = jnp.zeros((seqs, MARGIN, HD), BF16)
        v_buf[:, MARGIN + toks :, :HD] = jnp.zeros((seqs, MARGIN, HD), BF16)
        k1[:, 32 + cells :, :] = jnp.zeros((seqs, 32, HD), F32)
        v1[:, 32 + cells :, :] = jnp.zeros((seqs, 32, HD), F32)

    pl.semaphore_wait(barrier, cubes + n_head - 1 + outer_there.astype(jnp.int32))

    def token_copy(side):
        rows = pl.ds(0, BLK) if side == 0 else pl.ds(2 * toks - BLK, BLK)
        return pltpu.make_async_remote_copy(
            src_ref=kv_hbm.at[:, rows, :],
            dst_ref=tok_recv.at[1 - side],
            send_sem=tok_ssem.at[side],
            recv_sem=tok_rsem.at[1 - side],
            device_id=(me - 1 if side == 0 else me + 1, head),
            device_id_type=MESH,
        )

    def cells_copy(side):
        return pltpu.make_async_remote_copy(
            src_ref=cells_send.at[side],
            dst_ref=cells_recv.at[1 - side],
            send_sem=cells_ssem.at[side],
            recv_sem=cells_rsem.at[1 - side],
            device_id=(me - 1 if side == 0 else me + 1, head),
            device_id_type=MESH,
        )

    there = (has_low, has_high)
    for side in range(2):

        @pl.when(there[side])
        def _(side=side):
            token_copy(side).start()

    def split_chunk(source, s, dst):
        parts = dot_nn(splitter[...], source)
        k_buf[s, pl.ds(dst, MARGIN), :] = parts[:MARGIN].astype(BF16)
        v_buf[s, pl.ds(dst, MARGIN), :HD] = parts[MARGIN:BLK].astype(BF16)
        return parts

    for s in range(seqs):
        pltpu.make_async_copy(kv_hbm.at[s], raw.at[s], kv_sem.at[s]).wait()

        def chunk(j, carry, s=s):
            start = pl.multiple_of(j * BLK, BLK)
            dst = pl.multiple_of(j * MARGIN + MARGIN, MARGIN)
            parts = split_chunk(raw[s, pl.ds(start, BLK), :], s, dst)
            at = pl.multiple_of(j * 8 + 32, 8)
            k1[s, pl.ds(at, 8), :] = parts[BLK : BLK + 8].astype(BF16).astype(F32)
            v1[s, pl.ds(at, 8), :] = parts[BLK + 8 :].astype(BF16).astype(F32)
            return carry

        lax.fori_loop(0, 2 * toks // BLK, chunk, 0, unroll=4)

    for side in range(2):
        at = 32 if side == 0 else cells
        for s in range(seqs):
            cells_send[side, s, :32, :] = k1[s, at : at + 32, :].astype(BF16)
            cells_send[side, s, 32:, :] = v1[s, at : at + 32, :].astype(BF16)

        @pl.when(there[side])
        def _(side=side):
            cells_copy(side).start()

    pool_row = iota((CELL, 2 * cells), 0)
    pool_col = iota((CELL, 2 * cells), 1)
    pool_two = jnp.where(pool_col // CELL == pool_row, 1.0 / CELL, 0.0).astype(BF16)
    for s in range(seqs):
        ones_kv = jnp.concatenate(
            [k1[s, 32 : 32 + cells, :], v1[s, 32 : 32 + cells, :]], axis=0
        ).astype(BF16)
        pair[core, s] = dot_nn(pool_two, ones_kv).astype(BF16)
    pair_copy = pltpu.make_async_remote_copy(
        src_ref=pair.at[core],
        dst_ref=pair.at[core],
        send_sem=pair_ssem,
        recv_sem=pair_rsem,
        device_id=(me + 1 - 2 * core, head),
        device_id_type=MESH,
    )
    pair_copy.start()
    pair_copy.wait()

    def cube_copy(slot):
        target = chip + 2 - core - slot
        return pltpu.make_async_remote_copy(
            src_ref=pair,
            dst_ref=cube_recv.at[slot],
            send_sem=cube_ssem.at[slot],
            recv_sem=cube_rsem.at[slot],
            device_id=(target * 2 + core, head),
            device_id_type=MESH,
        )

    def cube_goes(slot):
        target = chip + 2 - core - slot
        return (target >= 0) & (target < cubes) & (slot != 2 - core)

    def cube_comes(slot):
        source = chip - 2 + core + slot
        return (source >= 0) & (source < cubes) & (slot != 2 - core)

    for s in range(seqs):
        both = pair[0, s].astype(F32) + pair[1, s].astype(F32)
        for half in range(2):
            mean = jnp.sum(both[8 * half : 8 * half + 8], axis=0, keepdims=True) / CELL
            third_send[2 * s + half : 2 * s + half + 1, :] = mean.astype(BF16).astype(F32)

    def third_copy(k):
        return pltpu.make_async_remote_copy(
            src_ref=third_send,
            dst_ref=third.at[pl.ds((cubes - 1 - k) * 8, 8), :],
            send_sem=third_ssem.at[k],
            recv_sem=third_rsem.at[cubes - 1 - k],
            device_id=((chip + k) % cubes * 2 + core, head),
            device_id_type=MESH,
        )

    for k in range(1, cubes):
        third_copy(k).start()
    for slot in range(4):

        @pl.when(cube_goes(slot))
        def _(slot=slot):
            cube_copy(slot).start()

    for k in range(1, cubes):
        third_copy(k).wait_recv()
    for s in range(seqs):
        k23[s, 64:, :] = third[pl.ds(2 * s, 16, stride=8), :]
        v23[s, 64:, :] = third[pl.ds(2 * s + 1, 16, stride=8), :]
    for slot in range(4):
        for half in range(2):
            at = slot * 16 + half * 8

            @pl.when(slot == 2 - core)
            def _(half=half, at=at):
                for s in range(seqs):
                    tile = pair[half, s].astype(F32)
                    k23[s, at : at + 8, :] = tile[:8]
                    v23[s, at : at + 8, :] = tile[8:]

            @pl.when(cube_comes(slot))
            def _(slot=slot, half=half, at=at):
                if half == 0:
                    cube_copy(slot).wait_recv()
                for s in range(seqs):
                    tile = cube_recv[slot, half, s].astype(F32)
                    k23[s, at : at + 8, :] = tile[:8]
                    v23[s, at : at + 8, :] = tile[8:]

    lane = iota((1, EXTRA), 1)
    ones_row = jnp.ones((16, HD), BF16)
    ones_tile = jnp.ones((EXTRA, HD), BF16)

    def extra_bias(b):
        start = dev_start + b * BLK
        first_lo = start - 2 * BLK
        first_hi = start + 3 * BLK
        second_lo = (first_lo + CUBE) // CUBE * CUBE - 2 * CUBE
        second_hi = (first_hi + CUBE - 1) // CUBE * CUBE + CUBE
        one_pos = jnp.where(
            lane < LOW, first_lo + lane * CELL, start + 384 + (lane - LOW) * CELL
        )
        two_pos = ((chip - 2 + core) * 16 + lane - 2 * LOW) * BLK
        third_slot = lane - 112
        third_cube = (chip + 1 + third_slot) % cubes
        three_pos = third_cube * CUBE
        one_ok = (one_pos >= 0) & (one_pos < seq_len)
        two_ok = (
            (two_pos >= 0)
            & (two_pos < seq_len)
            & (two_pos >= second_lo)
            & (two_pos < second_hi)
            & ((two_pos < first_lo) | (two_pos >= first_hi))
        )
        three_ok = (third_slot < cubes - 1) & (
            (three_pos < second_lo) | (three_pos >= second_hi)
        )
        return jnp.where(
            lane < 2 * LOW,
            jnp.where(one_ok, LEVEL_STEP, NEG),
            jnp.where(
                lane < 112,
                jnp.where(two_ok, 2 * LEVEL_STEP, NEG),
                jnp.where(three_ok, 3 * LEVEL_STEP, NEG),
            ),
        )

    def near_bias(b):
        pos = dev_start + b * BLK - MARGIN + iota((1, NEAR), 1)
        return jnp.where((pos >= 0) & (pos < seq_len), 0.0, NEG)

    def attend(s, b, edge):
        at = pl.multiple_of(b * BLK, BLK)
        cell_at = pl.multiple_of(b * CELL, CELL)
        q = q_buf[s, pl.ds(at, BLK), :]
        near_k = k_buf[s, pl.ds(at, NEAR), :]
        near_v = v_buf[s, pl.ds(at, NEAR), :]

        def extras(one, rest):
            return jnp.concatenate(
                [
                    one[s, pl.ds(cell_at, LOW), :],
                    one[s, pl.ds(pl.multiple_of(cell_at + 56, 8), LOW), :],
                    rest[s],
                ],
                axis=0,
            ).astype(BF16)

        extra_k = extras(k1, k23)
        extra_v = jnp.concatenate([extras(v1, v23), ones_tile], axis=1)
        near_s = dot_nt(q, near_k)
        if edge:
            near_s = near_s + near_bias(b)
        extra_s = dot_nt(q, extra_k) + extra_bias(b)
        top = jnp.maximum(
            jnp.max(near_s, axis=1, keepdims=True),
            jnp.max(extra_s, axis=1, keepdims=True),
        )
        near_w = jnp.exp2((near_s - top) * EXP_SCALE).astype(BF16)
        extra_w = jnp.exp2((extra_s - top) * EXP_SCALE).astype(BF16)
        out = dot_nn(near_w, near_v) + dot_nn(extra_w, extra_v)
        result = (out[:, :HD] / out[:, HD:]).astype(BF16)
        att[s, pl.ds(at, BLK), :] = result
        wide = result.astype(F32)
        square = dot_nt(ones_row, (wide * wide).astype(BF16))
        own_sum[b, 2 * s : 2 * s + 1, :] = square[:1, :HD]
        own_sum[b, 2 * s + 1 : 2 * s + 2, :] = square[:1, HD:]

    def att_copy(b):
        rows = pl.ds(pl.multiple_of(b * BLK, BLK), BLK)
        return pltpu.make_async_copy(
            att.at[:, rows, :], att_hbm.at[:, rows, :], out_sem.at[b]
        )

    def sum_copy(b, k):
        return pltpu.make_async_remote_copy(
            src_ref=own_sum.at[b],
            dst_ref=sums.at[b, n_head - 1 - k],
            send_sem=sum_ssem.at[b, k],
            recv_sem=sum_rsem.at[b, n_head - 1 - k],
            device_id=(me, (head + k) % n_head),
            device_id_type=MESH,
        )

    def run_block(b, edge):
        for s in range(seqs):
            attend(s, b, edge)
        att_copy(b).start()
        for k in range(1, n_head):
            sum_copy(b, k).start()

    for s in range(seqs):
        pltpu.make_async_copy(q_hbm.at[s], q_buf.at[s], q_sem.at[s]).wait()

    def inner(b, carry):
        run_block(b, False)
        return carry

    lax.fori_loop(2, blocks - 2, inner, 0)

    for side in range(2):

        @pl.when(there[side])
        def _(side=side):
            cells_copy(1 - side).wait_recv()
            at = 0 if side == 0 else 32 + cells
            for s in range(seqs):
                k1[s, at : at + 32, :] = cells_recv[side, s, :32, :].astype(F32)
                v1[s, at : at + 32, :] = cells_recv[side, s, 32:, :].astype(F32)

    def second_inner(i, carry):
        run_block(1 + i * (blocks - 3), False)
        return carry

    lax.fori_loop(0, 2, second_inner, 0)

    for side in range(2):

        @pl.when(there[side])
        def _(side=side):
            token_copy(1 - side).wait_recv()
            at = 0 if side == 0 else MARGIN + toks
            for s in range(seqs):
                split_chunk(tok_recv[side, s], s, at)

    def outermost(i, carry):
        run_block(i * (blocks - 1), True)
        return carry

    lax.fori_loop(0, 2, outermost, 0)

    def add_up(b, carry):
        acc = own_sum[b]
        for k in range(1, n_head):
            sum_copy(b, k).wait_recv()
        for k in range(n_head - 1):
            acc = acc + sums[b, k]
        total[b] = acc
        return carry

    lax.fori_loop(0, blocks, add_up, 0)
    total_copy = pltpu.make_async_copy(total, total_hbm, out_sem.at[blocks])
    total_copy.start()

    def drain(b, carry):
        att_copy(b).wait()
        for k in range(1, n_head):
            sum_copy(b, k).wait_send()
        return carry

    lax.fori_loop(0, blocks, drain, 0)
    for side in range(2):

        @pl.when(there[side])
        def _(side=side):
            token_copy(side).wait_send()
            cells_copy(side).wait_send()

    for slot in range(4):

        @pl.when(cube_goes(slot))
        def _(slot=slot):
            cube_copy(slot).wait_send()

    for k in range(1, cubes):
        third_copy(k).wait_send()
    total_copy.wait()


def attention(queries, pairs, n_seq, n_head):
    seqs, toks, _ = queries.shape
    blocks = toks // BLK
    cells = toks // CELL
    cubes = n_seq // 2
    assert toks == CUBE // 2 and cubes <= 16 and 2 * seqs <= 8
    vmem = pltpu.VMEM
    dma = pltpu.SemaphoreType.DMA
    hbm = pl.BlockSpec(memory_space=pl.ANY)
    return pl.pallas_call(
        functools.partial(fmm_kernel, n_seq, n_head),
        out_shape=(
            jax.ShapeDtypeStruct((seqs, toks, HD), BF16),
            jax.ShapeDtypeStruct((blocks, 8, HD), F32),
        ),
        in_specs=[hbm, hbm],
        out_specs=(hbm, hbm),
        scratch_shapes=[
            vmem((seqs, 2 * toks, HD), BF16),
            vmem((seqs, toks, HD), BF16),
            vmem((seqs, toks + BLK, HD), BF16),
            vmem((seqs, toks + BLK, 2 * HD), BF16),
            vmem((seqs, cells + 64, HD), F32),
            vmem((seqs, cells + 64, HD), F32),
            vmem((seqs, 80, HD), F32),
            vmem((seqs, 80, HD), F32),
            vmem((2, seqs, BLK, HD), BF16),
            vmem((2, seqs, 64, HD), BF16),
            vmem((2, seqs, 64, HD), BF16),
            vmem((2, seqs, CELL, HD), BF16),
            vmem((4, 2, seqs, CELL, HD), BF16),
            vmem((8, HD), F32),
            vmem((16 * 8, HD), F32),
            vmem((seqs, toks, HD), BF16),
            vmem((blocks, 8, HD), F32),
            vmem((blocks, n_head - 1, 8, HD), F32),
            vmem((blocks, 8, HD), F32),
            vmem((ROWS, BLK), BF16),
            dma((seqs,)),
            dma((seqs,)),
            dma((blocks + 1,)),
            dma((2,)),
            dma((2,)),
            dma((2,)),
            dma((2,)),
            dma(()),
            dma(()),
            dma((4,)),
            dma((4,)),
            dma((16,)),
            dma((16,)),
            dma((blocks, n_head)),
            dma((blocks, n_head)),
        ],
        compiler_params=pltpu.CompilerParams(
            collective_id=0, has_side_effects=True, vmem_limit_bytes=56 * 2**20
        ),
        cost_estimate=pl.CostEstimate(
            flops=4 * seqs * toks * 640 * HD,
            bytes_accessed=8 * seqs * toks * HD,
            transcendentals=seqs * toks * 640,
        ),
    )(queries, pairs)


def on_device(n_seq, n_head, queries, keys_values, norm_gain):
    seqs, toks, width = queries.shape
    pairs = keys_values.reshape(seqs, 2 * toks, width)
    att, total = attention(queries, pairs, n_seq, n_head)
    blocks = toks // BLK
    square_sum = total[:, : 2 * seqs].reshape(blocks, seqs, BLK)
    square_sum = jnp.transpose(square_sum, (1, 0, 2)).reshape(seqs, toks)
    scale_row = 1.0 / jnp.sqrt(square_sum / (HD * n_head) + 1e-06)
    return (att.astype(F32) * scale_row[..., None] * norm_gain).astype(BF16)


def solution(mesh):
    n_seq, n_head = mesh.shape["seq"], mesh.shape["head"]
    in_specs = (P(None, "seq", "head"), P(None, "seq", None, "head"), P("head"))
    return jax.shard_map(
        functools.partial(on_device, n_seq, n_head),
        mesh=mesh,
        in_specs=in_specs,
        out_specs=P(None, "seq", "head"),
        check_vma=False,
    )
```

time: 183 us -> 57.1 us (0.31)
  the two profiles are of different devices: /device:TPU:100 before, /device:TPU:4 now
where the time goes in v1:
time: 57.1 us; the launch traced here: 56.9 us
  Pallas kernels  52.6 us (92%)
  other arithmetic  4.22 us (7%)
    pallas_call x1, Pallas kernels, attention(): pl.pallas_call(functools.partial(fmm_kernel, n_seq, n_head), out_shape=(j...  52.6 us
    convert_element_type x1, other arithmetic, on_device(): return (att.astype(F32) * scale_row[..., None] * norm_gain).astype(BF16)  3.45 us

profile of v1, /device:TPU:4, one launch (start us, length us, event | category | flops | bytes accessed | tf_op | source)
XLA Modules:
  0.0 56.9 jit_solution(10145824723228074354)
XLA Ops:
  0.0 0.0 copy-start
  0.0 52.6 %shard_map.37 = (bf16[4,2048,128]{2,1,0:T(8,128)(2,1)}, f32[8,8,128]{2,1,0:T(8,128)}) custom-call(bf16[4,2048,128]{2,1,0:T(8,128)(2,1)} %q_hbm.1, bf16[4,4096,128]{2,1,0:T(8,128)(2,1)} %bitcast.5), custom_call_target="tpu_custom_call" | custom-call | flops 2684354560 | bytes 8388608 | tf_op jit(solution)/shard_map/pallas_call | solution.py:489
  52.6 0.8 %add_rsqrt_fusion = f32[8,8,128]{2,1,0:T(8,128)S(1)} fusion(f32[8,8,128]{2,1,0:T(8,128)} %get-tuple-element.8), kind=kLoop, calls=%fused_computation.1 | loop fusion | flops 16384 | bytes 65536 | tf_op jit(solution)/shard_map/sqrt | solution.py:552
  53.4 0.0 copy-done
  53.5 3.4 %multiply_convert_fusion = bf16[4,2048,128]{2,1,0:T(8,128)(2,1)} fusion(bf16[4,2048,128]{2,1,0:T(8,128)(2,1)} %get-tuple-element.7, f32[128]{0:T(128)S(1)} %copy-done, f32[4,2048]{1,0:T(4,128)S(1)} %bitcast.4), kind=kLoop, calls=%fused_computation | loop fusion | flops 4194304 | bytes 4227584 | tf_op jit(solution)/shard_map/convert_element_type | solution.py:553
  (1 shorter events, 0.0 us)
Async XLA Ops:
  0.0 53.4 %copy-start = (f32[128]{0:T(128)S(1)}, f32[128]{0:T(128)}, u32[]{:S(2)}) copy-start(f32[128]{0:T(128)} %param.5) | copy-start | bytes 1540

commit v2 on v1

v2 whole, which is shorter than its diff:
```python
import functools
import math

import jax
import jax.numpy as jnp
from jax import lax
from jax.experimental import pallas as pl
from jax.experimental.pallas import tpu as pltpu
from jax.sharding import PartitionSpec as P

HD = 128
CELL = 16
BLK = 256
CUBE = 4096
MARGIN = 128
NEAR = 512
LOW = 24
EXTRA = 128
TWO_PASS = (6, 3)
EARLY = 2
NEG = -1e30
EXP_SCALE = math.log2(math.e) / math.sqrt(HD)
LEVEL_STEP = 2.0 / EXP_SCALE
MESH = pl.DeviceIdType.MESH
F32 = jnp.float32
BF16 = jnp.bfloat16


def dot_nt(a, b):
    return lax.dot_general(a, b, (((1,), (1,)), ((), ())), preferred_element_type=F32)


def dot_nn(a, b):
    return lax.dot_general(a, b, (((1,), (0,)), ((), ())), preferred_element_type=F32)


def iota(shape, dim):
    return lax.broadcasted_iota(jnp.int32, shape, dim)


def split_matrix():
    row = iota((BLK, BLK), 0)
    col = iota((BLK, BLK), 1)
    return (col == 2 * (row % MARGIN) + row // MARGIN).astype(BF16)


def pool_matrix():
    row = iota((CELL, BLK), 0)
    col = iota((CELL, BLK), 1)
    picked = (col // (2 * CELL) == row % 8) & (col % 2 == row // 8)
    return jnp.where(picked, 1.0 / CELL, 0.0).astype(BF16)


def fmm_kernel(
    n_seq,
    n_head,
    q_hbm,
    kv_hbm,
    gain_ref,
    att,
    raw,
    q_buf,
    k_buf,
    v_buf,
    k1,
    v1,
    k23,
    v23,
    tok_recv,
    cells_send,
    cells_recv,
    pair,
    cube_recv,
    third_send,
    third,
    near_out,
    near_top,
    own_sum,
    sums,
    splitter,
    q_sem,
    kv_sem,
    tok_ssem,
    tok_rsem,
    cells_ssem,
    cells_rsem,
    pair_ssem,
    pair_rsem,
    cube_ssem,
    cube_rsem,
    third_ssem,
    third_rsem,
    sum_ssem,
    sum_rsem,
):
    seqs, toks, _ = q_hbm.shape
    blocks = toks // BLK
    cells = toks // CELL
    cubes = n_seq // 2
    seq_len = n_seq * toks
    me = lax.axis_index("seq")
    head = lax.axis_index("head")
    core = me % 2
    chip = me // 2
    dev_start = me * toks
    parts = ((0, blocks - 2), (blocks - 2, 2))
    first_half = me < n_seq // 2
    early = jnp.where(first_half, EARLY, 0)
    two_pass = jnp.where(first_half, *TWO_PASS)
    has_low = me > 0
    has_high = me < n_seq - 1

    for s in range(seqs):
        pltpu.make_async_copy(kv_hbm.at[s], raw.at[s], kv_sem.at[s]).start()
    for s in range(seqs):
        pltpu.make_async_copy(q_hbm.at[s], q_buf.at[s], q_sem.at[s]).start()

    barrier = pltpu.get_barrier_semaphore()

    def greet(seq_id, head_id):
        pl.semaphore_signal(
            barrier, inc=1, device_id=(seq_id, head_id), device_id_type=MESH
        )

    greet(me + 1 - 2 * core, head)
    for k in range(1, cubes):
        greet((chip + k) % cubes * 2 + core, head)
    for k in range(1, n_head):
        greet(me, (head + k) % n_head)
    outer = me - 1 + 2 * core
    outer_there = (outer >= 0) & (outer < n_seq)

    @pl.when(outer_there)
    def _():
        greet(outer, head)

    splitter[...] = split_matrix()
    v_buf[:, :, HD:] = jnp.ones((seqs, toks + BLK, HD), BF16)
    spare = 16 - (cubes - 1)
    third[(cubes - 1) * 8 :, :] = jnp.zeros((spare * 8, HD), F32)
    k23[...] = jnp.zeros_like(k23)
    v23[...] = jnp.zeros_like(v23)

    @pl.when(jnp.logical_not(has_low))
    def _():
        k_buf[:, :MARGIN, :] = jnp.zeros((seqs, MARGIN, HD), BF16)
        v_buf[:, :MARGIN, :HD] = jnp.zeros((seqs, MARGIN, HD), BF16)
        k1[:, :32, :] = jnp.zeros((seqs, 32, HD), F32)
        v1[:, :32, :] = jnp.zeros((seqs, 32, HD), F32)

    @pl.when(jnp.logical_not(has_high))
    def _():
        k_buf[:, MARGIN + toks :, :] = jnp.zeros((seqs, MARGIN, HD), BF16)
        v_buf[:, MARGIN + toks :, :HD] = jnp.zeros((seqs, MARGIN, HD), BF16)
        k1[:, 32 + cells :, :] = jnp.zeros((seqs, 32, HD), F32)
        v1[:, 32 + cells :, :] = jnp.zeros((seqs, 32, HD), F32)


    def token_copy(side):
        rows = pl.ds(0, BLK) if side == 0 else pl.ds(2 * toks - BLK, BLK)
        return pltpu.make_async_remote_copy(
            src_ref=kv_hbm.at[:, rows, :],
            dst_ref=tok_recv.at[1 - side],
            send_sem=tok_ssem.at[side],
            recv_sem=tok_rsem.at[1 - side],
            device_id=(me - 1 if side == 0 else me + 1, head),
            device_id_type=MESH,
        )

    def cells_copy(side):
        return pltpu.make_async_remote_copy(
            src_ref=cells_send.at[side],
            dst_ref=cells_recv.at[1 - side],
            send_sem=cells_ssem.at[side],
            recv_sem=cells_rsem.at[1 - side],
            device_id=(me - 1 if side == 0 else me + 1, head),
            device_id_type=MESH,
        )

    there = (has_low, has_high)
    pooler = pool_matrix()
    for s in range(seqs):
        pltpu.make_async_copy(kv_hbm.at[s], raw.at[s], kv_sem.at[s]).wait()

        def pool_chunk(j, carry, s=s):
            start = pl.multiple_of(j * BLK, BLK)
            cell = dot_nn(pooler, raw[s, pl.ds(start, BLK), :])
            at = pl.multiple_of(j * 8 + 32, 8)
            k1[s, pl.ds(at, 8), :] = cell[:8].astype(BF16).astype(F32)
            v1[s, pl.ds(at, 8), :] = cell[8:].astype(BF16).astype(F32)
            return carry

        lax.fori_loop(0, 2 * toks // BLK, pool_chunk, 0, unroll=16)

    def split_chunk(source, s, dst):
        parts = dot_nn(splitter[...], source)
        k_buf[s, pl.ds(dst, MARGIN), :] = parts[:MARGIN].astype(BF16)
        v_buf[s, pl.ds(dst, MARGIN), :HD] = parts[MARGIN:].astype(BF16)

    def loop_split(i, carry):
        for s in range(seqs):
            for j in range(2):
                chunk = i * 2 + j
                start = pl.multiple_of(chunk * BLK, BLK)
                dst = pl.multiple_of(chunk * MARGIN + MARGIN, MARGIN)
                split_chunk(raw[s, pl.ds(start, BLK), :], s, dst)
        return carry

    split_steps = toks // BLK
    split_first = jnp.where(first_half, split_steps, 0)

    pool_row = iota((CELL, 2 * cells), 0)
    pool_col = iota((CELL, 2 * cells), 1)
    pool_two = jnp.where(pool_col // CELL == pool_row, 1.0 / CELL, 0.0).astype(BF16)
    for s in range(seqs):
        ones_kv = jnp.concatenate(
            [k1[s, 32 : 32 + cells, :], v1[s, 32 : 32 + cells, :]], axis=0
        ).astype(BF16)
        pair[core, s] = dot_nn(pool_two, ones_kv).astype(BF16)
    pair_copy = pltpu.make_async_remote_copy(
        src_ref=pair.at[core],
        dst_ref=pair.at[core],
        send_sem=pair_ssem,
        recv_sem=pair_rsem,
        device_id=(me + 1 - 2 * core, head),
        device_id_type=MESH,
    )
    for side in range(2):
        at = 32 if side == 0 else cells
        for s in range(seqs):
            cells_send[side, s, :32, :] = k1[s, at : at + 32, :].astype(BF16)
            cells_send[side, s, 32:, :] = v1[s, at : at + 32, :].astype(BF16)

    def cube_copy(slot):
        target = chip + 2 - core - slot
        return pltpu.make_async_remote_copy(
            src_ref=pair,
            dst_ref=cube_recv.at[slot],
            send_sem=cube_ssem.at[slot],
            recv_sem=cube_rsem.at[slot],
            device_id=(target * 2 + core, head),
            device_id_type=MESH,
        )

    def cube_goes(slot):
        target = chip + 2 - core - slot
        return (target >= 0) & (target < cubes) & (slot != 2 - core)

    def cube_comes(slot):
        source = chip - 2 + core + slot
        return (source >= 0) & (source < cubes) & (slot != 2 - core)

    def third_copy(k):
        return pltpu.make_async_remote_copy(
            src_ref=third_send,
            dst_ref=third.at[pl.ds((cubes - 1 - k) * 8, 8), :],
            send_sem=third_ssem.at[k],
            recv_sem=third_rsem.at[cubes - 1 - k],
            device_id=((chip + k) % cubes * 2 + core, head),
            device_id_type=MESH,
        )

    lane = iota((1, EXTRA), 1)
    ones_tile = jnp.ones((EXTRA, HD), BF16)
    eye = iota((HD, HD), 0) == iota((HD, HD), 1)

    def extra_bias(b):
        start = dev_start + b * BLK
        first_lo = start - 2 * BLK
        first_hi = start + 3 * BLK
        second_lo = (first_lo + CUBE) // CUBE * CUBE - 2 * CUBE
        second_hi = (first_hi + CUBE - 1) // CUBE * CUBE + CUBE
        one_pos = jnp.where(
            lane < LOW, first_lo + lane * CELL, start + 384 + (lane - LOW) * CELL
        )
        two_pos = ((chip - 2 + core) * 16 + lane - 2 * LOW) * BLK
        third_slot = lane - 112
        third_cube = (chip + 1 + third_slot) % cubes
        three_pos = third_cube * CUBE
        one_ok = (one_pos >= 0) & (one_pos < seq_len)
        two_ok = (
            (two_pos >= 0)
            & (two_pos < seq_len)
            & (two_pos >= second_lo)
            & (two_pos < second_hi)
            & ((two_pos < first_lo) | (two_pos >= first_hi))
        )
        three_ok = (third_slot < cubes - 1) & (
            (three_pos < second_lo) | (three_pos >= second_hi)
        )
        return jnp.where(
            lane < 2 * LOW,
            jnp.where(one_ok, LEVEL_STEP, NEG),
            jnp.where(
                lane < 112,
                jnp.where(two_ok, 2 * LEVEL_STEP, NEG),
                jnp.where(three_ok, 3 * LEVEL_STEP, NEG),
            ),
        )

    def near_bias(b):
        pos = dev_start + b * BLK - MARGIN + iota((1, NEAR), 1)
        return jnp.where((pos >= 0) & (pos < seq_len), 0.0, NEG)

    def near_scores(s, b):
        at = pl.multiple_of(b * BLK, BLK)
        return dot_nt(q_buf[s, pl.ds(at, BLK), :], k_buf[s, pl.ds(at, NEAR), :])

    def extra_scores(s, b, bias):
        at = pl.multiple_of(b * BLK, BLK)
        return dot_nt(q_buf[s, pl.ds(at, BLK), :], extras(k1, k23, s, b)) + bias

    def near_values(s, b):
        return v_buf[s, pl.ds(pl.multiple_of(b * BLK, BLK), NEAR), :]

    def extra_values(s, b):
        return jnp.concatenate([extras(v1, v23, s, b), ones_tile], axis=1)

    def weigh(score, top):
        return jnp.exp2((score - top) * EXP_SCALE).astype(BF16)

    def extras(one, rest, s, b):
        cell_at = pl.multiple_of(b * CELL, CELL)
        return jnp.concatenate(
            [
                one[s, pl.ds(cell_at, LOW), :],
                one[s, pl.ds(pl.multiple_of(cell_at + 56, 8), LOW), :],
                rest[s],
            ],
            axis=0,
        ).astype(BF16)

    def near_part(b, place):
        scores = [near_scores(s, b) for s in range(seqs)]
        tops = [jnp.max(score, axis=1, keepdims=True) for score in scores]
        for s in range(seqs):
            near_out[place, s] = dot_nn(weigh(scores[s], tops[s]), near_values(s, b))
            near_top[place, s] = jnp.broadcast_to(tops[s], (BLK, HD))

    def finish(s, b, place, summed, row_total):
        at = pl.multiple_of(b * BLK, BLK)
        result = (summed / row_total).astype(BF16)
        att[s, pl.ds(at, BLK), :] = result
        wide = result.astype(F32)
        square = jnp.sum(wide * wide, axis=1, keepdims=True)
        for half in range(2):
            picked = jnp.where(eye, square[half * HD : half * HD + HD], 0.0)
            row = 2 * s + half
            own_sum[place, row : row + 1, :] = jnp.sum(picked, axis=0, keepdims=True)

    def far_part(b, place):
        bias = extra_bias(b)
        scores = [extra_scores(s, b, bias) for s in range(seqs)]
        for s in range(seqs):
            near = near_top[place, s]
            top = jnp.maximum(near, jnp.max(scores[s], axis=1, keepdims=True))
            shrink = jnp.exp2((near - top) * EXP_SCALE)
            part = dot_nn(weigh(scores[s], top), extra_values(s, b))
            summed = near_out[place, s, :, :HD] * shrink + part[:, :HD]
            row_total = near_out[place, s, :, HD:] * shrink + part[:, HD:]
            finish(s, b, place, summed, row_total)

    def whole_part(b, place, edge):
        bias = extra_bias(b)
        near = [near_scores(s, b) for s in range(seqs)]
        if edge:
            outside = near_bias(b)
            near = [score + outside for score in near]
        far = [extra_scores(s, b, bias) for s in range(seqs)]
        tops = [
            jnp.maximum(
                jnp.max(near[s], axis=1, keepdims=True),
                jnp.max(far[s], axis=1, keepdims=True),
            )
            for s in range(seqs)
        ]
        outs = [
            dot_nn(weigh(near[s], tops[s]), near_values(s, b))
            + dot_nn(weigh(far[s], tops[s]), extra_values(s, b))
            for s in range(seqs)
        ]
        for s in range(seqs):
            finish(s, b, place, outs[s][:, :HD], outs[s][:, HD:])

    def sum_copy(part, k):
        places = pl.ds(*parts[part])
        return pltpu.make_async_remote_copy(
            src_ref=own_sum.at[places],
            dst_ref=sums.at[n_head - 1 - k, places],
            send_sem=sum_ssem.at[part, k],
            recv_sem=sum_rsem.at[part, n_head - 1 - k],
            device_id=(me, (head + k) % n_head),
            device_id_type=MESH,
        )

    def block_at(place):
        inner_end = blocks - 4
        return jnp.where(
            place < inner_end,
            place + 2,
            jnp.where(
                place < inner_end + 2,
                1 + (place - inner_end) * (blocks - 3),
                (place - inner_end - 2) * (blocks - 1),
            ),
        )

    def normalize(place, carry):
        b = block_at(place)
        acc = own_sum[place]
        for k in range(n_head - 1):
            acc = acc + sums[k, place]
        scale = jnp.transpose(1.0 / jnp.sqrt(acc / (HD * n_head) + 1e-06))
        gain = gain_ref[...]
        for s in range(seqs):
            for half in range(2):
                at = pl.multiple_of(b * BLK + half * HD, HD)
                column = scale[:, 2 * s + half : 2 * s + half + 1]
                wide = att[s, pl.ds(at, HD), :].astype(F32)
                att[s, pl.ds(at, HD), :] = (wide * column * gain).astype(BF16)
        return carry

    def loop_near(place, carry):
        near_part(block_at(place), place)
        return carry

    def loop_far(place, carry):
        far_part(block_at(place), place)
        return carry

    def loop_whole(place, carry):
        whole_part(block_at(place), place, False)
        return carry

    def loop_edge(place, carry):
        whole_part(block_at(place), place, True)
        return carry

    def q_wait():
        for s in range(seqs):
            pltpu.make_async_copy(q_hbm.at[s], q_buf.at[s], q_sem.at[s]).wait()

    q_wait()
    lax.fori_loop(0, split_first, loop_split, 0)
    lax.fori_loop(0, early, loop_near, 0)
    pl.semaphore_wait(barrier, cubes + n_head - 1 + outer_there.astype(jnp.int32))
    pair_copy.start()
    lax.fori_loop(split_first, split_steps, loop_split, 0)
    pair_copy.wait()
    for s in range(seqs):
        both = pair[0, s].astype(F32) + pair[1, s].astype(F32)
        for half in range(2):
            mean = jnp.sum(both[8 * half : 8 * half + 8], axis=0, keepdims=True) / CELL
            third_send[2 * s + half : 2 * s + half + 1, :] = mean.astype(BF16).astype(F32)

    for k in range(1, cubes):
        third_copy(k).start()
    for slot in range(4):

        @pl.when(cube_goes(slot))
        def _(slot=slot):
            cube_copy(slot).start()

    for side in range(2):

        @pl.when(there[side])
        def _(side=side):
            cells_copy(side).start()
            token_copy(side).start()

    lax.fori_loop(early, two_pass, loop_near, 0)

    for side in range(2):

        @pl.when(there[side])
        def _(side=side):
            cells_copy(1 - side).wait_recv()
            at = 0 if side == 0 else 32 + cells
            for s in range(seqs):
                k1[s, at : at + 32, :] = cells_recv[side, s, :32, :].astype(F32)
                v1[s, at : at + 32, :] = cells_recv[side, s, 32:, :].astype(F32)

    for k in range(1, cubes):
        third_copy(k).wait_recv()
    for s in range(seqs):
        k23[s, 64:, :] = third[pl.ds(2 * s, 16, stride=8), :]
        v23[s, 64:, :] = third[pl.ds(2 * s + 1, 16, stride=8), :]
    for slot in range(4):
        for half in range(2):
            at = slot * 16 + half * 8

            @pl.when(slot == 2 - core)
            def _(half=half, at=at):
                for s in range(seqs):
                    tile = pair[half, s].astype(F32)
                    k23[s, at : at + 8, :] = tile[:8]
                    v23[s, at : at + 8, :] = tile[8:]

            @pl.when(cube_comes(slot))
            def _(slot=slot, half=half, at=at):
                if half == 0:
                    cube_copy(slot).wait_recv()
                for s in range(seqs):
                    tile = cube_recv[slot, half, s].astype(F32)
                    k23[s, at : at + 8, :] = tile[:8]
                    v23[s, at : at + 8, :] = tile[8:]

    lax.fori_loop(0, two_pass, loop_far, 0)
    lax.fori_loop(two_pass, blocks - 2, loop_whole, 0)
    for k in range(1, n_head):
        sum_copy(0, k).start()

    for side in range(2):

        @pl.when(there[side])
        def _(side=side):
            token_copy(1 - side).wait_recv()
            at = 0 if side == 0 else MARGIN + toks
            for s in range(seqs):
                split_chunk(tok_recv[side, s], s, at)

    lax.fori_loop(blocks - 2, blocks, loop_edge, 0)
    for k in range(1, n_head):
        sum_copy(1, k).start()
    for k in range(1, n_head):
        sum_copy(0, k).wait_recv()
    lax.fori_loop(0, blocks - 2, normalize, 0)
    for k in range(1, n_head):
        sum_copy(1, k).wait_recv()
    lax.fori_loop(blocks - 2, blocks, normalize, 0)

    for part in range(2):
        for k in range(1, n_head):
            sum_copy(part, k).wait_send()
    for side in range(2):

        @pl.when(there[side])
        def _(side=side):
            token_copy(side).wait_send()
            cells_copy(side).wait_send()

    for slot in range(4):

        @pl.when(cube_goes(slot))
        def _(slot=slot):
            cube_copy(slot).wait_send()

    for k in range(1, cubes):
        third_copy(k).wait_send()


def attention(queries, pairs, gain, n_seq, n_head):
    seqs, toks, _ = queries.shape
    blocks = toks // BLK
    cells = toks // CELL
    cubes = n_seq // 2
    assert toks == CUBE // 2 and cubes <= 16 and 2 * seqs <= 8
    vmem = pltpu.VMEM
    dma = pltpu.SemaphoreType.DMA
    hbm = pl.BlockSpec(memory_space=pl.ANY)
    return pl.pallas_call(
        functools.partial(fmm_kernel, n_seq, n_head),
        out_shape=vmem((seqs, toks, HD), BF16),
        in_specs=[hbm, hbm, pl.BlockSpec(memory_space=vmem)],
        out_specs=pl.BlockSpec(memory_space=vmem),
        scratch_shapes=[
            vmem((seqs, 2 * toks, HD), BF16),
            vmem((seqs, toks, HD), BF16),
            vmem((seqs, toks + BLK, HD), BF16),
            vmem((seqs, toks + BLK, 2 * HD), BF16),
            vmem((seqs, cells + 64, HD), F32),
            vmem((seqs, cells + 64, HD), F32),
            vmem((seqs, 80, HD), F32),
            vmem((seqs, 80, HD), F32),
            vmem((2, seqs, BLK, HD), BF16),
            vmem((2, seqs, 64, HD), BF16),
            vmem((2, seqs, 64, HD), BF16),
            vmem((2, seqs, CELL, HD), BF16),
            vmem((4, 2, seqs, CELL, HD), BF16),
            vmem((8, HD), F32),
            vmem((16 * 8, HD), F32),
            vmem((max(TWO_PASS), seqs, BLK, 2 * HD), F32),
            vmem((max(TWO_PASS), seqs, BLK, HD), F32),
            vmem((blocks, 8, HD), F32),
            vmem((n_head - 1, blocks, 8, HD), F32),
            vmem((BLK, BLK), BF16),
            dma((seqs,)),
            dma((seqs,)),
            dma((2,)),
            dma((2,)),
            dma((2,)),
            dma((2,)),
            dma(()),
            dma(()),
            dma((4,)),
            dma((4,)),
            dma((16,)),
            dma((16,)),
            dma((2, n_head)),
            dma((2, n_head)),
        ],
        compiler_params=pltpu.CompilerParams(
            collective_id=0, has_side_effects=True, vmem_limit_bytes=61 * 2**20
        ),
        cost_estimate=pl.CostEstimate(
            flops=4 * seqs * toks * 640 * HD,
            bytes_accessed=8 * seqs * toks * HD,
            transcendentals=seqs * toks * 640,
        ),
    )(queries, pairs, gain)


def on_device(n_seq, n_head, queries, keys_values, norm_gain):
    seqs, toks, width = queries.shape
    pairs = keys_values.reshape(seqs, 2 * toks, width)
    return attention(queries, pairs, norm_gain.reshape(1, HD), n_seq, n_head)


def solution(mesh):
    n_seq, n_head = mesh.shape["seq"], mesh.shape["head"]
    in_specs = (P(None, "seq", "head"), P(None, "seq", None, "head"), P("head"))
    return jax.shard_map(
        functools.partial(on_device, n_seq, n_head),
        mesh=mesh,
        in_specs=in_specs,
        out_specs=P(None, "seq", "head"),
        check_vma=False,
    )
```

time: 57.1 us -> 35.9 us (0.63)
  the two profiles are of different devices: /device:TPU:4 before, /device:TPU:65 now
where the time goes in v2:
time: 35.9 us; the launch traced here: 35.8 us
  Pallas kernels  34.5 us (96%)
  local copies, waits for them, and re-layouts  1.32 us (4%)
    pallas_call x1, Pallas kernels, attention(): pl.pallas_call(functools.partial(fmm_kernel, n_seq, n_head), out_shape=vm...  34.5 us
    unnamed x1, local copies, waits for them, and re-layouts  1.32 us

profile of v2, /device:TPU:65, one launch (start us, length us, event | category | flops | bytes accessed | tf_op | source)
XLA Modules:
  0.0 35.8 jit_solution(9363484011569310808)
XLA Ops:
  0.0 34.5 %shard_map.37 = bf16[4,2048,128]{2,1,0:T(8,128)(2,1)S(1)} custom-call(bf16[4,2048,128]{2,1,0:T(8,128)(2,1)} %q_hbm.1, bf16[4,4096,128]{2,1,0:T(8,128)(2,1)} %bitcast.2, f32[1,128]{1,0:T(1,128)} %bitcast.3), custom_call_target="tpu_custom_call" | custom-call | flops 2684354560 | bytes 8388608 | tf_op jit(solution)/shard_map/pallas_call | solution.py:561
  34.5 1.3 %copy.5 = bf16[4,2048,128]{2,1,0:T(8,128)(2,1)} copy(bf16[4,2048,128]{2,1,0:T(8,128)(2,1)S(1)} %shard_map.37) | data formatting | bytes 4194304

commit v3 on v2

--- a/solution.py
+++ b/solution.py
@@ -16,8 +16,8 @@
 NEAR = 512
 LOW = 24
 EXTRA = 128
-TWO_PASS = (6, 3)
-EARLY = 2
+TWO_PASS = (3, 1)
+EARLY = 1
 NEG = -1e30
 EXP_SCALE = math.log2(math.e) / math.sqrt(HD)
 LEVEL_STEP = 2.0 / EXP_SCALE
@@ -192,18 +192,21 @@
 
         lax.fori_loop(0, 2 * toks // BLK, pool_chunk, 0, unroll=16)
 
-    def split_chunk(source, s, dst):
-        parts = dot_nn(splitter[...], source)
-        k_buf[s, pl.ds(dst, MARGIN), :] = parts[:MARGIN].astype(BF16)
-        v_buf[s, pl.ds(dst, MARGIN), :HD] = parts[MARGIN:].astype(BF16)
+    def split_chunks(sources, places):
+        parts = dot_nn(splitter[...], jnp.concatenate(sources, axis=1))
+        for i, (s, dst) in enumerate(places):
+            mine = parts[:, i * HD : i * HD + HD].astype(BF16)
+            k_buf[s, pl.ds(dst, MARGIN), :] = mine[:MARGIN]
+            v_buf[s, pl.ds(dst, MARGIN), :HD] = mine[MARGIN:]
 
     def loop_split(i, carry):
         for s in range(seqs):
-            for j in range(2):
-                chunk = i * 2 + j
-                start = pl.multiple_of(chunk * BLK, BLK)
-                dst = pl.multiple_of(chunk * MARGIN + MARGIN, MARGIN)
-                split_chunk(raw[s, pl.ds(start, BLK), :], s, dst)
+            start = pl.multiple_of(i * 2 * BLK, 2 * BLK)
+            dst = pl.multiple_of(i * BLK + MARGIN, MARGIN)
+            split_chunks(
+                [raw[s, pl.ds(start, BLK), :], raw[s, pl.ds(start + BLK, BLK), :]],
+                [(s, dst), (s, dst + MARGIN)],
+            )
         return carry
 
     split_steps = toks // BLK
@@ -330,12 +333,15 @@
             axis=0,
         ).astype(BF16)
 
-    def near_part(b, place):
-        scores = [near_scores(s, b) for s in range(seqs)]
+    def items_of(places):
+        return [(s, block_at(place), place) for place in places for s in range(seqs)]
+
+    def near_part(items):
+        scores = [near_scores(s, b) for s, b, _ in items]
         tops = [jnp.max(score, axis=1, keepdims=True) for score in scores]
-        for s in range(seqs):
-            near_out[place, s] = dot_nn(weigh(scores[s], tops[s]), near_values(s, b))
-            near_top[place, s] = jnp.broadcast_to(tops[s], (BLK, HD))
+        for (s, b, place), score, top in zip(items, scores, tops):
+            near_out[place, s] = dot_nn(weigh(score, top), near_values(s, b))
+            near_top[place, s] = jnp.broadcast_to(top, (BLK, HD))
 
     def finish(s, b, place, summed, row_total):
         at = pl.multiple_of(b * BLK, BLK)
@@ -348,39 +354,40 @@
             row = 2 * s + half
             own_sum[place, row : row + 1, :] = jnp.sum(picked, axis=0, keepdims=True)
 
-    def far_part(b, place):
-        bias = extra_bias(b)
-        scores = [extra_scores(s, b, bias) for s in range(seqs)]
-        for s in range(seqs):
-            near = near_top[place, s]
-            top = jnp.maximum(near, jnp.max(scores[s], axis=1, keepdims=True))
-            shrink = jnp.exp2((near - top) * EXP_SCALE)
-            part = dot_nn(weigh(scores[s], top), extra_values(s, b))
+    def far_part(items):
+        scores = [extra_scores(s, b, extra_bias(b)) for s, b, _ in items]
+        tops = [
+            jnp.maximum(near_top[place, s], jnp.max(score, axis=1, keepdims=True))
+            for (s, _, place), score in zip(items, scores)
+        ]
+        parts = [
+            dot_nn(weigh(score, top), extra_values(s, b))
+            for (s, b, _), score, top in zip(items, scores, tops)
+        ]
+        for (s, b, place), part, top in zip(items, parts, tops):
+            shrink = jnp.exp2((near_top[place, s] - top) * EXP_SCALE)
             summed = near_out[place, s, :, :HD] * shrink + part[:, :HD]
             row_total = near_out[place, s, :, HD:] * shrink + part[:, HD:]
             finish(s, b, place, summed, row_total)
 
-    def whole_part(b, place, edge):
-        bias = extra_bias(b)
-        near = [near_scores(s, b) for s in range(seqs)]
+    def whole_part(items, edge):
+        near = [near_scores(s, b) for s, b, _ in items]
         if edge:
-            outside = near_bias(b)
-            near = [score + outside for score in near]
-        far = [extra_scores(s, b, bias) for s in range(seqs)]
+            near = [x + near_bias(b) for x, (_, b, _) in zip(near, items)]
+        far = [extra_scores(s, b, extra_bias(b)) for s, b, _ in items]
         tops = [
             jnp.maximum(
-                jnp.max(near[s], axis=1, keepdims=True),
-                jnp.max(far[s], axis=1, keepdims=True),
+                jnp.max(x, axis=1, keepdims=True), jnp.max(y, axis=1, keepdims=True)
             )
-            for s in range(seqs)
+            for x, y in zip(near, far)
         ]
         outs = [
-            dot_nn(weigh(near[s], tops[s]), near_values(s, b))
-            + dot_nn(weigh(far[s], tops[s]), extra_values(s, b))
-            for s in range(seqs)
+            dot_nn(weigh(x, top), near_values(s, b))
+            + dot_nn(weigh(y, top), extra_values(s, b))
+            for (s, b, _), x, y, top in zip(items, near, far, tops)
         ]
-        for s in range(seqs):
-            finish(s, b, place, outs[s][:, :HD], outs[s][:, HD:])
+        for (s, b, place), out in zip(items, outs):
+            finish(s, b, place, out[:, :HD], out[:, HD:])
 
     def sum_copy(part, k):
         places = pl.ds(*parts[part])
@@ -410,38 +417,40 @@
         acc = own_sum[place]
         for k in range(n_head - 1):
             acc = acc + sums[k, place]
-        scale = jnp.transpose(1.0 / jnp.sqrt(acc / (HD * n_head) + 1e-06))
+        scale = 1.0 / jnp.sqrt(acc / (HD * n_head) + 1e-06)
         gain = gain_ref[...]
         for s in range(seqs):
             for half in range(2):
                 at = pl.multiple_of(b * BLK + half * HD, HD)
-                column = scale[:, 2 * s + half : 2 * s + half + 1]
+                row = 2 * s + half
+                picked = jnp.where(eye, scale[row : row + 1], 0.0)
+                column = jnp.sum(picked, axis=1, keepdims=True)
                 wide = att[s, pl.ds(at, HD), :].astype(F32)
                 att[s, pl.ds(at, HD), :] = (wide * column * gain).astype(BF16)
         return carry
 
-    def loop_near(place, carry):
-        near_part(block_at(place), place)
+    def loop_near(i, carry):
+        near_part(items_of((2 * i, 2 * i + 1)))
         return carry
 
-    def loop_far(place, carry):
-        far_part(block_at(place), place)
+    def loop_far(i, carry):
+        far_part(items_of((2 * i, 2 * i + 1)))
         return carry
 
-    def loop_whole(place, carry):
-        whole_part(block_at(place), place, False)
+    def loop_whole(i, carry):
+        whole_part(items_of((2 * i, 2 * i + 1)), False)
         return carry
 
-    def loop_edge(place, carry):
-        whole_part(block_at(place), place, True)
+    def loop_edge(i, carry):
+        whole_part(items_of((2 * i, 2 * i + 1)), True)
         return carry
 
     def q_wait():
         for s in range(seqs):
             pltpu.make_async_copy(q_hbm.at[s], q_buf.at[s], q_sem.at[s]).wait()
 
+    lax.fori_loop(0, split_first, loop_split, 0)
     q_wait()
-    lax.fori_loop(0, split_first, loop_split, 0)
     lax.fori_loop(0, early, loop_near, 0)
     pl.semaphore_wait(barrier, cubes + n_head - 1 + outer_there.astype(jnp.int32))
     pair_copy.start()
@@ -506,7 +515,7 @@
                     v23[s, at : at + 8, :] = tile[8:]
 
     lax.fori_loop(0, two_pass, loop_far, 0)
-    lax.fori_loop(two_pass, blocks - 2, loop_whole, 0)
+    lax.fori_loop(two_pass, blocks // 2 - 1, loop_whole, 0)
     for k in range(1, n_head):
         sum_copy(0, k).start()
 
@@ -516,10 +525,13 @@
         def _(side=side):
             token_copy(1 - side).wait_recv()
             at = 0 if side == 0 else MARGIN + toks
-            for s in range(seqs):
-                split_chunk(tok_recv[side, s], s, at)
-
-    lax.fori_loop(blocks - 2, blocks, loop_edge, 0)
+            for s in range(0, seqs, 2):
+                pair_of = range(s, min(s + 2, seqs))
+                split_chunks(
+                    [tok_recv[side, i] for i in pair_of], [(i, at) for i in pair_of]
+                )
+
+    lax.fori_loop(blocks // 2 - 1, blocks // 2, loop_edge, 0)
     for k in range(1, n_head):
         sum_copy(1, k).start()
     for k in range(1, n_head):
@@ -579,8 +591,8 @@
             vmem((4, 2, seqs, CELL, HD), BF16),
             vmem((8, HD), F32),
             vmem((16 * 8, HD), F32),
-            vmem((max(TWO_PASS), seqs, BLK, 2 * HD), F32),
-            vmem((max(TWO_PASS), seqs, BLK, HD), F32),
+            vmem((2 * max(TWO_PASS), seqs, BLK, 2 * HD), F32),
+            vmem((2 * max(TWO_PASS), seqs, BLK, HD), F32),
             vmem((blocks, 8, HD), F32),
             vmem((n_head - 1, blocks, 8, HD), F32),
             vmem((BLK, BLK), BF16),

time: 35.9 us -> 33.2 us (0.925)
  Pallas kernels: 34.5 us -> 31.8 us
    pallas_call x1, Pallas kernels: 34.5 us -> 31.8 us  [attention(): pl.pallas_call(functools.partial(fmm_kernel, n_seq, n_head), out_shape=vm...]
where the time goes in v3:
time: 33.2 us; the launch traced here: 33.1 us
  Pallas kernels  31.8 us (96%)
  local copies, waits for them, and re-layouts  1.32 us (4%)
    pallas_call x1, Pallas kernels, attention(): pl.pallas_call(functools.partial(fmm_kernel, n_seq, n_head), out_shape=vm...  31.8 us
    unnamed x1, local copies, waits for them, and re-layouts  1.32 us

profile of v3, /device:TPU:65, one launch (start us, length us, event | category | flops | bytes accessed | tf_op | source)
XLA Modules:
  0.0 33.1 jit_solution(4928589723407315353)
XLA Ops:
  0.0 31.8 %shard_map.37 = bf16[4,2048,128]{2,1,0:T(8,128)(2,1)S(1)} custom-call(bf16[4,2048,128]{2,1,0:T(8,128)(2,1)} %q_hbm.1, bf16[4,4096,128]{2,1,0:T(8,128)(2,1)} %bitcast.2, f32[1,128]{1,0:T(1,128)} %bitcast.3), custom_call_target="tpu_custom_call" | custom-call | flops 2684354560 | bytes 8388608 | tf_op jit(solution)/shard_map/pallas_call | solution.py:573
  31.8 1.3 %copy.5 = bf16[4,2048,128]{2,1,0:T(8,128)(2,1)} copy(bf16[4,2048,128]{2,1,0:T(8,128)(2,1)S(1)} %shard_map.37) | data formatting | bytes 4194304

commit v4 on v3

--- a/solution.py
+++ b/solution.py
@@ -16,8 +16,9 @@
 NEAR = 512
 LOW = 24
 EXTRA = 128
-TWO_PASS = (3, 1)
+TWO_PASS = (3, 2)
 EARLY = 1
+SPLIT_THEN = 3
 NEG = -1e30
 EXP_SCALE = math.log2(math.e) / math.sqrt(HD)
 LEVEL_STEP = 2.0 / EXP_SCALE
@@ -105,7 +106,7 @@
     dev_start = me * toks
     parts = ((0, blocks - 2), (blocks - 2, 2))
     first_half = me < n_seq // 2
-    early = jnp.where(first_half, EARLY, 0)
+    early = jnp.where(first_half & (chip % 2 == 0), EARLY, 0)
     two_pass = jnp.where(first_half, *TWO_PASS)
     has_low = me > 0
     has_high = me < n_seq - 1
@@ -301,10 +302,6 @@
             ),
         )
 
-    def near_bias(b):
-        pos = dev_start + b * BLK - MARGIN + iota((1, NEAR), 1)
-        return jnp.where((pos >= 0) & (pos < seq_len), 0.0, NEG)
-
     def near_scores(s, b):
         at = pl.multiple_of(b * BLK, BLK)
         return dot_nt(q_buf[s, pl.ds(at, BLK), :], k_buf[s, pl.ds(at, NEAR), :])
@@ -354,26 +351,69 @@
             row = 2 * s + half
             own_sum[place, row : row + 1, :] = jnp.sum(picked, axis=0, keepdims=True)
 
+    def merge(items, scores, values):
+        tops = [
+            jnp.maximum(near_top[slot, s], jnp.max(score, axis=1, keepdims=True))
+            for (s, _, _, slot), score in zip(items, scores)
+        ]
+        parts = [
+            dot_nn(weigh(score, top), values(s, b))
+            for (s, b, _, _), score, top in zip(items, scores, tops)
+        ]
+        for (s, b, place, slot), part, top in zip(items, parts, tops):
+            shrink = jnp.exp2((near_top[slot, s] - top) * EXP_SCALE)
+            summed = near_out[slot, s, :, :HD] * shrink + part[:, :HD]
+            row_total = near_out[slot, s, :, HD:] * shrink + part[:, HD:]
+            finish(s, b, place, summed, row_total)
+
     def far_part(items):
         scores = [extra_scores(s, b, extra_bias(b)) for s, b, _ in items]
+        merge([(s, b, place, place) for s, b, place in items], scores, extra_values)
+
+    def halo_at(b):
+        return pl.multiple_of(jnp.where(b == 0, 0, MARGIN + toks), MARGIN)
+
+    def edge_local(items):
+        span = NEAR - MARGIN
+        near = []
+        for s, b, _ in items:
+            at = pl.multiple_of(b * BLK, BLK)
+            local = pl.multiple_of(at + jnp.where(b == 0, MARGIN, 0), MARGIN)
+            keys = k_buf[s, pl.ds(local, span), :]
+            near.append(dot_nt(q_buf[s, pl.ds(at, BLK), :], keys))
+        far = [extra_scores(s, b, extra_bias(b)) for s, b, _ in items]
         tops = [
-            jnp.maximum(near_top[place, s], jnp.max(score, axis=1, keepdims=True))
-            for (s, _, place), score in zip(items, scores)
+            jnp.maximum(
+                jnp.max(x, axis=1, keepdims=True), jnp.max(y, axis=1, keepdims=True)
+            )
+            for x, y in zip(near, far)
         ]
-        parts = [
-            dot_nn(weigh(score, top), extra_values(s, b))
-            for (s, b, _), score, top in zip(items, scores, tops)
-        ]
-        for (s, b, place), part, top in zip(items, parts, tops):
-            shrink = jnp.exp2((near_top[place, s] - top) * EXP_SCALE)
-            summed = near_out[place, s, :, :HD] * shrink + part[:, :HD]
-            row_total = near_out[place, s, :, HD:] * shrink + part[:, HD:]
-            finish(s, b, place, summed, row_total)
-
-    def whole_part(items, edge):
+        for (s, b, place), x, y, top in zip(items, near, far, tops):
+            at = b * BLK + jnp.where(b == 0, MARGIN, 0)
+            values = v_buf[s, pl.ds(pl.multiple_of(at, MARGIN), span), :]
+            slot = place - (blocks - 2)
+            near_out[slot, s] = dot_nn(weigh(x, top), values) + dot_nn(
+                weigh(y, top), extra_values(s, b)
+            )
+            near_top[slot, s] = jnp.broadcast_to(top, (BLK, HD))
+
+    def halo_scores(s, b):
+        at = pl.multiple_of(b * BLK, BLK)
+        pos = dev_start + halo_at(b) - MARGIN + iota((1, MARGIN), 1)
+        bias = jnp.where((pos >= 0) & (pos < seq_len), 0.0, NEG)
+        keys = k_buf[s, pl.ds(halo_at(b), MARGIN), :]
+        return dot_nt(q_buf[s, pl.ds(at, BLK), :], keys) + bias
+
+    def halo_values(s, b):
+        return v_buf[s, pl.ds(halo_at(b), MARGIN), :]
+
+    def edge_halo(items):
+        scores = [halo_scores(s, b) for s, b, _ in items]
+        with_slots = [(s, b, place, place - (blocks - 2)) for s, b, place in items]
+        merge(with_slots, scores, halo_values)
+
+    def whole_part(items):
         near = [near_scores(s, b) for s, b, _ in items]
-        if edge:
-            near = [x + near_bias(b) for x, (_, b, _) in zip(near, items)]
         far = [extra_scores(s, b, extra_bias(b)) for s, b, _ in items]
         tops = [
             jnp.maximum(
@@ -438,11 +478,15 @@
         return carry
 
     def loop_whole(i, carry):
-        whole_part(items_of((2 * i, 2 * i + 1)), False)
+        whole_part(items_of((2 * i, 2 * i + 1)))
         return carry
 
+    def loop_local(i, carry):
+        edge_local(items_of((2 * i, 2 * i + 1)))
+        return carry
+
     def loop_edge(i, carry):
-        whole_part(items_of((2 * i, 2 * i + 1)), True)
+        edge_halo(items_of((2 * i, 2 * i + 1)))
         return carry
 
     def q_wait():
@@ -450,11 +494,16 @@
             pltpu.make_async_copy(q_hbm.at[s], q_buf.at[s], q_sem.at[s]).wait()
 
     lax.fori_loop(0, split_first, loop_split, 0)
-    q_wait()
+
+    @pl.when(first_half)
+    def _():
+        q_wait()
+
     lax.fori_loop(0, early, loop_near, 0)
     pl.semaphore_wait(barrier, cubes + n_head - 1 + outer_there.astype(jnp.int32))
     pair_copy.start()
-    lax.fori_loop(split_first, split_steps, loop_split, 0)
+    split_then = jnp.where(first_half, split_steps, SPLIT_THEN)
+    lax.fori_loop(split_first, split_then, loop_split, 0)
     pair_copy.wait()
     for s in range(seqs):
         both = pair[0, s].astype(F32) + pair[1, s].astype(F32)
@@ -476,6 +525,12 @@
         def _(side=side):
             cells_copy(side).start()
             token_copy(side).start()
+
+    lax.fori_loop(split_then, split_steps, loop_split, 0)
+
+    @pl.when(jnp.logical_not(first_half))
+    def _():
+        q_wait()
 
     lax.fori_loop(early, two_pass, loop_near, 0)
 
@@ -519,6 +574,7 @@
     for k in range(1, n_head):
         sum_copy(0, k).start()
 
+    lax.fori_loop(blocks // 2 - 1, blocks // 2, loop_local, 0)
     for side in range(2):
 
         @pl.when(there[side])

time: 33.2 us -> 32.7 us (0.985)
  the two profiles are of different devices: /device:TPU:65 before, /device:TPU:100 now
where the time goes in v4:
time: 32.7 us; the launch traced here: 32.6 us
  Pallas kernels  31.3 us (96%)
  local copies, waits for them, and re-layouts  1.32 us (4%)
    pallas_call x1, Pallas kernels, attention(): pl.pallas_call(functools.partial(fmm_kernel, n_seq, n_head), out_shape=vm...  31.3 us
    unnamed x1, local copies, waits for them, and re-layouts  1.32 us

profile of v4, /device:TPU:100, one launch (start us, length us, event | category | flops | bytes accessed | tf_op | source)
XLA Modules:
  0.0 32.6 jit_solution(9619134666172896175)
XLA Ops:
  0.0 31.3 %shard_map.37 = bf16[4,2048,128]{2,1,0:T(8,128)(2,1)S(1)} custom-call(bf16[4,2048,128]{2,1,0:T(8,128)(2,1)} %q_hbm.1, bf16[4,4096,128]{2,1,0:T(8,128)(2,1)} %bitcast.2, f32[1,128]{1,0:T(1,128)} %bitcast.3), custom_call_target="tpu_custom_call" | custom-call | flops 2684354560 | bytes 8388608 | tf_op jit(solution)/shard_map/pallas_call | solution.py:629
  31.3 1.3 %copy.5 = bf16[4,2048,128]{2,1,0:T(8,128)(2,1)} copy(bf16[4,2048,128]{2,1,0:T(8,128)(2,1)S(1)} %shard_map.37) | data formatting | bytes 4194304

commit v5 on v4

--- a/solution.py
+++ b/solution.py
@@ -113,8 +113,6 @@
 
     for s in range(seqs):
         pltpu.make_async_copy(kv_hbm.at[s], raw.at[s], kv_sem.at[s]).start()
-    for s in range(seqs):
-        pltpu.make_async_copy(q_hbm.at[s], q_buf.at[s], q_sem.at[s]).start()
 
     barrier = pltpu.get_barrier_semaphore()
 
@@ -192,6 +190,9 @@
             return carry
 
         lax.fori_loop(0, 2 * toks // BLK, pool_chunk, 0, unroll=16)
+
+    for s in range(seqs):
+        pltpu.make_async_copy(q_hbm.at[s], q_buf.at[s], q_sem.at[s]).start()
 
     def split_chunks(sources, places):
         parts = dot_nn(splitter[...], jnp.concatenate(sources, axis=1))

time: 32.7 us -> 32.5 us (level)
  no operation moved by 1% of the time
where the time goes in v5:
time: 32.5 us; the launch traced here: 32.4 us
  Pallas kernels  31 us (95%)
  local copies, waits for them, and re-layouts  1.32 us (4%)
    pallas_call x1, Pallas kernels, attention(): pl.pallas_call(functools.partial(fmm_kernel, n_seq, n_head), out_shape=vm...  31 us
    unnamed x1, local copies, waits for them, and re-layouts  1.32 us

profile of v5, /device:TPU:100, one launch (start us, length us, event | category | flops | bytes accessed | tf_op | source)
XLA Modules:
  0.0 32.4 jit_solution(13432835477492806049)
XLA Ops:
  0.0 31.0 %shard_map.37 = bf16[4,2048,128]{2,1,0:T(8,128)(2,1)S(1)} custom-call(bf16[4,2048,128]{2,1,0:T(8,128)(2,1)} %q_hbm.1, bf16[4,4096,128]{2,1,0:T(8,128)(2,1)} %bitcast.2, f32[1,128]{1,0:T(1,128)} %bitcast.3), custom_call_target="tpu_custom_call" | custom-call | flops 2684354560 | bytes 8388608 | tf_op jit(solution)/shard_map/pallas_call | solution.py:630
  31.0 1.3 %copy.5 = bf16[4,2048,128]{2,1,0:T(8,128)(2,1)} copy(bf16[4,2048,128]{2,1,0:T(8,128)(2,1)S(1)} %shard_map.37) | data formatting | bytes 4194304
